TPU v7x, 32 devices: a whole 2x2x4 slice. The times are simulated.
32 devices in a mesh: dp: 16 (over z, x, core), node: 2 (over y).
Axes of the slice: x: 2, y: 2, z: 4, core: 2. Of those that a mesh axis runs over, the one named last changes fastest.
Arguments:
- hidden_in: bfloat16 [4096, 4096], P(('dp', 'node')), may hold values from -6 to 6
- norm_gain: float32 [4096], replicated, may hold values from 0.1 to 1.9
- key_weight: bfloat16 [4096, 1024], P('dp', 'node'), may hold values from -0.09375 to 0.09375
- value_weight: bfloat16 [4096, 1024], P('dp', 'node'), may hold values from -0.09375 to 0.09375
- queries: bfloat16 [4096, 2048], P('dp', 'node'), may hold values from -240 to 240
- out_cotangent: bfloat16 [4096, 2048], P('dp', 'node'), may hold values from -6 to 6
Outputs:
- attention: bfloat16 [4096, 2048], P('dp', 'node')
- key_grad: float32 [4096, 1024], P('dp', 'node')
All inputs are finite; a program needn't handle non-finite values.
Results may differ from a plain program's by a relative error of at most 0.0065.
The roundings to bfloat16 on the way count: a program that leaves them out, or rounds other values in their place, can miss the bound.
Values may be sent and summed in bfloat16 or wider, within the bound.
A program may use at most 64 MiB of HBM per device.

v0:
```python
import jax
import jax.numpy as jnp
from jax import lax
from jax.sharding import PartitionSpec as P

HEADS = 16
KV_HEADS = 8
HD = 128


epsilon = 1e-05


def rms_normalize(hidden_rows, norm_gain):
    widened = hidden_rows.astype(jnp.float32)
    inverse = lax.rsqrt(jnp.mean(widened * widened, axis=-1, keepdims=True) + epsilon)
    return (widened * inverse * norm_gain).astype(jnp.bfloat16)


def local(hidden_in, norm_gain, key_weight, value_weight, queries, out_cotangent):
    local_width = key_weight.shape[1]
    kv_local = local_width // HD
    group_size = HEADS // KV_HEADS
    score_scale = HD ** (-0.5)
    gathered = lax.all_gather(hidden_in, "node", axis=0, tiled=True)
    normed = rms_normalize(gathered, norm_gain)
    seq_rows = normed.shape[0]

    def add_rows(shard_piece):
        return jnp.dot(normed, shard_piece, preferred_element_type=jnp.float32)

    key_sum = add_rows(lax.all_gather(key_weight, "dp", axis=0, tiled=True))
    value_sum = add_rows(lax.all_gather(value_weight, "dp", axis=0, tiled=True))
    key_proj = key_sum.astype(jnp.bfloat16).reshape(seq_rows, kv_local, HD)
    value_proj = value_sum.astype(jnp.bfloat16).reshape(seq_rows, kv_local, HD)
    block_rows = min(512, seq_rows)
    outputs = []
    grad_parts = []
    for block_index in range(seq_rows // block_rows):
        row_start = block_index * block_rows
        span_end = row_start + block_rows
        query_block = queries[row_start:span_end].reshape(block_rows, kv_local, group_size, HD)
        grad_block = out_cotangent[row_start:span_end].reshape(block_rows, kv_local, group_size, HD)
        key_window = key_proj[:span_end]
        value_window = value_proj[:span_end]
        scores = (
            jnp.einsum(
                "qkgd,skd->kgqs", query_block, key_window, preferred_element_type=jnp.float32
            )
            * score_scale
        )
        query_pos = row_start + jnp.arange(block_rows, dtype=jnp.int32)
        key_pos = jnp.arange(span_end, dtype=jnp.int32)
        allowed = query_pos[:, None] >= key_pos[None, :]
        scores = jnp.where(allowed, scores, -1e30)
        row_max = jnp.max(scores, axis=-1, keepdims=True)
        weights = jnp.exp(scores - row_max)
        probabilities = (weights / jnp.sum(weights, axis=-1, keepdims=True)).astype(jnp.bfloat16)
        attended = jnp.einsum(
            "kgqs,skd->qkgd", probabilities, value_window, preferred_element_type=jnp.float32
        )
        outputs.append(
            attended.astype(jnp.bfloat16).reshape(block_rows, kv_local * group_size * HD)
        )
        prob_grad = jnp.einsum(
            "qkgd,skd->kgqs", grad_block, value_window, preferred_element_type=jnp.float32
        )
        row_delta = jnp.sum(probabilities * prob_grad, axis=-1, keepdims=True)
        score_grad = (probabilities * (prob_grad - row_delta) * score_scale).astype(jnp.bfloat16)
        block_grad = jnp.einsum(
            "kgqs,qkgd->skd", score_grad, query_block, preferred_element_type=jnp.float32
        )
        grad_parts.append(jnp.pad(block_grad, ((0, seq_rows - span_end), (0, 0), (0, 0))))
    key_grad_acc = grad_parts[0]
    for extra_part in grad_parts[1:]:
        key_grad_acc = key_grad_acc + extra_part
    key_rows_grad = key_grad_acc.reshape(seq_rows, local_width).astype(jnp.bfloat16)
    key_grad = lax.psum_scatter(
        lax.dot_general(
            normed, key_rows_grad, (((0,), (0,)), ((), ())), preferred_element_type=jnp.float32
        ),
        "dp",
        scatter_dimension=0,
        tiled=True,
    )
    return (jnp.concatenate(outputs, axis=0), key_grad)


def solution(mesh):
    in_specs = (
        P(("dp", "node"), None),
        P(),
        P("dp", "node"),
        P("dp", "node"),
        P("dp", "node"),
        P("dp", "node"),
    )
    out_specs = (P("dp", "node"), P("dp", "node"))
    return jax.shard_map(local, mesh=mesh, in_specs=in_specs, out_specs=out_specs, check_vma=False)
```

profile of v0, /device:TPU:0, one launch (start us, length us, event | category | flops | bytes accessed | tf_op | source)
XLA Modules:
  0.0 281.3 jit_solution(16007617059810073825)
XLA Ops:
  7.2 0.0 copy-start.1
  7.2 0.0 all-gather.4.cloned.1.call-start
  7.2 0.7 all-gather.4.cloned.1.call-update
  7.9 0.0 all-gather.6.cloned.1.call-start
  8.0 0.7 all-gather.6.cloned.1.call-update
  8.7 0.0 all-gather.8.cloned.1.call-start
  8.7 0.7 all-gather.8.cloned.1.call-update
  9.4 0.0 copy-start.3
  9.4 0.0 reduce-scatter.2.cloned.1.call-start
  9.4 1.2 copy.29
  10.7 0.0 copy-done.1
  10.7 0.0 copy-start.2
  10.7 0.4 reshape.37
  11.1 34.3 %all-gather.4.cloned.1.call-done = bf16[256,4096]{1,0:T(8,128)(2,1)} async-done(((bf16[128,4096]{1,0:T(8,128)(2,1)}), bf16[256,4096]{1,0:T(8,128)(2,1)}) %all-gather.4.cloned.1.call-update) | async-done | bytes 2097168 | tf_op jit(solution)/shard_map/all_gather | solution.py:25
  45.4 0.0 copy-start
  45.4 2.2 fusion.2
  47.6 50.7 %all-gather.6.cloned.1.call-done = bf16[4096,512]{1,0:T(8,128)(2,1)} async-done(((bf16[256,512]{1,0:T(8,128)(2,1)}), bf16[4096,512]{1,0:T(8,128)(2,1)}) %all-gather.6.cloned.1.call-update) | async-done | bytes 4194320 | tf_op jit(solution)/shard_map/all_gather | solution.py:33
  98.3 0.0 copy-done.3
  98.3 0.0 copy-done
  98.3 4.2 %convolution_convert_fusion.2 = bf16[256,512]{1,0:T(8,128)(2,1)} fusion(bf16[4096,512]{1,0:T(8,128)(2,1)} %all-gather.6.cloned.1.call-done, bf16[256,4096]{1,0:T(8,128)(2,1)S(1)} %copy-done, f32[4096]{0:T(1024)S(1)} %copy-done.3, f32[256]{0:T(256)S(1)} %add_rsqrt_fusion), kind=kOutput, calls=%fused_computation.22 | convolution fusion | flops 1078067200 | bytes 6571008 | tf_op jit(solution)/shard_map/dot_general | solution.py:30
  102.5 1.0 reshape.33
  103.5 46.0 %all-gather.8.cloned.1.call-done = bf16[4096,512]{1,0:T(8,128)(2,1)} async-done(((bf16[256,512]{1,0:T(8,128)(2,1)}), bf16[4096,512]{1,0:T(8,128)(2,1)}) %all-gather.8.cloned.1.call-update) | async-done | bytes 4194320 | tf_op jit(solution)/shard_map/all_gather | solution.py:32
  149.6 4.2 %convolution_convert_fusion.1 = bf16[256,512]{1,0:T(8,128)(2,1)} fusion(bf16[4096,512]{1,0:T(8,128)(2,1)} %all-gather.8.cloned.1.call-done, bf16[256,4096]{1,0:T(8,128)(2,1)S(1)} %copy-done, f32[4096]{0:T(1024)S(1)} %copy-done.3, f32[256]{0:T(256)S(1)} %add_rsqrt_fusion), kind=kOutput, calls=%fused_computation.21 | convolution fusion | flops 1078067200 | bytes 6571008 | tf_op jit(solution)/shard_map/dot_general | solution.py:30
  153.8 1.7 reshape.34
  155.5 1.8 fusion.16
  157.2 0.0 copy-done.2
  157.2 3.1 %fusion.36 = (f32[4,2,256]{2,1,0:T(2,128)S(1)}, f32[4,2,256,256]{2,3,1,0:T(8,128)}) fusion(pred[256,256]{0,1:T(8,128)(4,1)S(1)} %iota_compare_fusion, bf16[256,4,2,128]{0,3,2,1:T(8,128)(2,1)S(1)} %bitcast.50, bf16[256,4,128,1]{2,1,0,3:T(4,128)(2,1)} %bitcast.53), kind=kOutput, calls=%fused_computation.40 | convolution fusion | flops 136315136 | bytes 2957312 | tf_op jit(solution)/shard_map/sub | solution.py:57
  160.3 1.8 divide_convert_fusion
  162.1 3.7 %fusion.11 = bf16[4,256,128]{1,2,0:T(8,128)(2,1)} fusion(bf16[256,4,2,128]{0,3,2,1:T(8,128)(2,1)} %bitcast.51, bf16[4,2,256,256]{2,3,1,0:T(8,128)(2,1)S(1)} %divide_convert_fusion, f32[4,256,256,2]{2,1,3,0:T(8,128)} %fusion.16), kind=kOutput, calls=%fused_computation.20 | convolution fusion | flops 138021120 | bytes 3932160 | tf_op jit(solution)/shard_map/kgqs,qkgd->skd/dot_general | solution.py:70
  165.8 5.6 %fusion.32 = f32[4096,512]{1,0:T(8,128)} fusion(bf16[256,512]{0,1:T(8,128)(2,1)} %bitcast.52, bf16[256,4096]{1,0:T(8,128)(2,1)S(1)} %copy-done, f32[4096]{0:T(1024)S(1)} %copy-done.3, f32[256]{0:T(256)S(1)} %add_rsqrt_fusion), kind=kOutput, calls=%fused_computation.39 | convolution fusion | flops 1077936128 | bytes 10765312 | tf_op jit(solution)/shard_map/dot_general | solution.py:79
  171.4 0.0 reduce-scatter.2.cloned.1.call-update
  171.4 0.3 convolution_convert_fusion
  171.8 1.0 copy.16
  172.8 102.0 %reduce-scatter.2.cloned.1.call-done = f32[256,512]{1,0:T(8,128)} async-done(((f32[4096,512]{1,0:T(8,128)}), f32[256,512]{1,0:T(8,128)}) %reduce-scatter.2.cloned.1.call-update) | async-done | bytes 524304 | tf_op jit(solution)/shard_map/reduce_scatter | solution.py:78
  (2 shorter events, 0.0 us)
Async XLA Ops:
  7.2 3.5 %copy-start.1 = (bf16[256,1024]{1,0:T(8,128)(2,1)S(1)}, bf16[256,1024]{1,0:T(8,128)(2,1)}, u32[]{:S(2)}) copy-start(bf16[256,1024]{1,0:T(8,128)(2,1)} %param.11) | copy-start | bytes 1572868
  7.2 38.2 %all-gather.4.cloned.1.call-start = ((), (), s32[]{:S(2)}) async-start(), calls=%async_computation.1 | async-start | bytes 3145728 | tf_op jit(solution)/shard_map/all_gather | solution.py:25
  7.9 90.4 %all-gather.6.cloned.1.call-start = ((), (), s32[]{:S(2)}) async-start(), calls=%async_computation.2 | async-start | bytes 4456448 | tf_op jit(solution)/shard_map/all_gather | solution.py:33
  8.7 140.9 %all-gather.8.cloned.1.call-start = ((), (), s32[]{:S(2)}) async-start(), calls=%async_computation.3 | async-start | bytes 4456448 | tf_op jit(solution)/shard_map/all_gather | solution.py:32
  9.4 88.9 %copy-start.3 = (f32[4096]{0:T(1024)S(1)}, f32[4096]{0:T(1024)}, u32[]{:S(2)}) copy-start(f32[4096]{0:T(1024)} %param.7) | copy-start | bytes 49156
  9.4 265.4 %reduce-scatter.2.cloned.1.call-start = ((), (), s32[]{:S(2)}) async-start(), calls=%async_computation.4 | async-start | bytes 8912896 | tf_op jit(solution)/shard_map/reduce_scatter | solution.py:78
  10.7 146.5 %copy-start.2 = (bf16[256,1024]{0,1:T(8,128)(2,1)}, bf16[256,1024]{0,1:T(8,128)(2,1)S(1)}, u32[]{:S(2)}) copy-start(bf16[256,1024]{0,1:T(8,128)(2,1)S(1)} %copy.29) | copy-start | bytes 1572868
  45.4 52.9 %copy-start = (bf16[256,4096]{1,0:T(8,128)(2,1)S(1)}, bf16[256,4096]{1,0:T(8,128)(2,1)}, u32[]{:S(2)}) copy-start(bf16[256,4096]{1,0:T(8,128)(2,1)} %all-gather.4.cloned.1.call-done) | copy-start | bytes 6291460
Sparse Core Ops, SparseCore 0:
  9.6 35.8 all-gather.3
  47.6 50.7 all-gather.5
  100.5 49.0 all-gather.7
  171.5 103.1 reduce-scatter.1
where the time goes:
time: 282 us; the launch traced here: 281 us
  waiting for transfers between devices  235 us (83%)
  matrix products  22.9 us (8%)
  between operations  13.8 us (5%)
  local copies, waits for them, and re-layouts  5.35 us (2%)
  other arithmetic  4.03 us (1%)
    reduce_scatter x1, waiting for transfers between devices, local(): lax.psum_scatter(lax.dot_general(normed, key_rows_grad, (((0,), (0,)), ((...  102 us
    all_gather x1, waiting for transfers between devices, local(): value_sum = add_rows(lax.all_gather(value_weight, 'dp', axis=0, tiled=True))  50.7 us
    all_gather x1, waiting for transfers between devices, local(): key_sum = add_rows(lax.all_gather(key_weight, 'dp', axis=0, tiled=True))  46 us
    all_gather x1, waiting for transfers between devices, local(): gathered = lax.all_gather(hidden_in, 'node', axis=0, tiled=True)  34.3 us
    dot_general x2, matrix products, add_rows(): return jnp.dot(normed, shard_piece, preferred_element_type=jnp.float32)  8.37 us
  transfers between devices with their start and end apart: 4, of which 4 were waited for; matrix products, arithmetic and copies ran while one was open for 4% of the time, Pallas kernels for 0%

commit v1 on v0

--- a/solution.py
+++ b/solution.py
@@ -1,6 +1,10 @@
+import functools
+
 import jax
 import jax.numpy as jnp
 from jax import lax
+from jax.experimental import pallas as pl
+from jax.experimental.pallas import tpu as pltpu
 from jax.sharding import PartitionSpec as P
 
 HEADS = 16
@@ -86,6 +90,256 @@
     return (jnp.concatenate(outputs, axis=0), key_grad)
 
 
+SUBS = 2
+EARLY = 5
+
+
+def dot(a, b):
+    return jnp.dot(a, b, preferred_element_type=jnp.float32)
+
+
+def dot_nt(a, b):
+    return lax.dot_general(a, b, (((1,), (1,)), ((), ())), preferred_element_type=jnp.float32)
+
+
+def dot_tn(a, b):
+    return lax.dot_general(a, b, (((0,), (0,)), ((), ())), preferred_element_type=jnp.float32)
+
+
+def kernel(ring, hidden, gain, kw, vw, queries, cotangent, attention, key_grad,
+           stage, act, slots, acc, part, kv, rows_grad, sums,
+           ag_send, ag_recv, act_send, act_recv, act_local, pair_send, pair_recv,
+           rs_send, rs_recv):
+    depth = ring // 2
+    steps = ring - 1
+    dp = lax.axis_index("dp")
+    node = lax.axis_index("node")
+    core = dp % 2
+    block = dp // 2
+    col = block % 2
+    row = block // 2
+    spot = row * (1 - col) + (2 * depth - 1 - row) * col
+
+    def block_at(position):
+        position = (position + 2 * ring) % ring
+        side = position // depth
+        level = position * (1 - side) + (2 * depth - 1 - position) * side
+        return level * 2 + side
+
+    right = (block_at(spot + 1) * 2 + core, node)
+    left = (block_at(spot - 1) * 2 + core, node)
+    sibling = (block * 2 + 1 - core, node)
+    beside = (dp, 1 - node)
+    across = (block * 2 + 1 - core, 1 - node)
+    mesh_ids = pl.DeviceIdType.MESH
+
+    barrier = pltpu.get_barrier_semaphore()
+    for peer in (right, left, sibling, beside, across):
+        pl.semaphore_signal(barrier, inc=1, device_id=peer, device_id_type=mesh_ids)
+    pl.semaphore_wait(barrier, 5)
+
+    def remote(source, target, send, recv, peer):
+        copy = pltpu.make_async_remote_copy(
+            src_ref=source, dst_ref=target, send_sem=send, recv_sem=recv,
+            device_id=peer, device_id_type=mesh_ids)
+        copy.start()
+        return copy
+
+    onward = (right, left)
+    features = kw.shape[0]
+    width = kw.shape[1]
+    cut = features // SUBS
+    started = []
+
+    def gather_copy(way, step, sub):
+        span = pl.ds(sub * cut, cut)
+        source = (kw, vw)[way].at[span] if step == 0 else slots.at[way, step - 1, span]
+        return remote(source, slots.at[way, step, span], ag_send.at[way, step, sub],
+                      ag_recv.at[way, step, sub], onward[way])
+
+    flight = {}
+    for sub in range(SUBS):
+        for way in range(2):
+            flight[way, 0, sub] = gather_copy(way, 0, sub)
+
+    own_rows = hidden.shape[0]
+    seq = 2 * own_rows
+    strip = 16
+
+    def normalize(index, carry):
+        rows = pl.ds(pl.multiple_of(index * strip, strip), strip)
+        wide = hidden[rows, :].astype(jnp.float32)
+        inverse = lax.rsqrt(jnp.mean(wide * wide, axis=-1, keepdims=True) + epsilon)
+        normed = (wide * inverse * gain[...]).astype(jnp.bfloat16)
+        for piece in range(2 * ring):
+            stage[piece % 2, piece // 2, rows, :] = normed[:, piece * features:(piece + 1) * features]
+        return carry
+
+    lax.fori_loop(0, own_rows // strip, normalize, 0)
+    my_rows = pl.ds(pl.multiple_of(core * seq + node * own_rows, own_rows), own_rows)
+    act_copies = []
+    for relation, (peer, plane) in enumerate(((across, 1 - core), (beside, core), (sibling, 1 - core))):
+        act_copies.append(remote(stage.at[plane], act.at[:, my_rows, :], act_send.at[relation],
+                                 act_recv.at[relation], peer))
+    local_copy = pltpu.make_async_copy(stage.at[core], act.at[:, my_rows, :], act_local)
+    local_copy.start()
+
+    def add_block(way, position, weight):
+        acc[way] = acc[way] + dot(act[block_at(position)], weight)
+
+    for step in range(1, steps + 1):
+        for sub in range(SUBS):
+            for way in range(2):
+                flight[way, step - 1, sub].wait_recv()
+                if step < steps:
+                    flight[way, step, sub] = gather_copy(way, step, sub)
+        if step == EARLY:
+            local_copy.wait()
+            for copy in act_copies:
+                copy.wait_recv()
+            acc[0] = dot(act[block], kw[...])
+            acc[1] = dot(act[block], vw[...])
+
+            def earlier(index, carry):
+                add_block(0, spot - 1 - index, slots[0, index])
+                add_block(1, spot + 1 + index, slots[1, index])
+                return carry
+
+            lax.fori_loop(0, EARLY, earlier, 0)
+        if step > EARLY:
+            add_block(0, spot - step, slots[0, step - 1])
+            add_block(1, spot + step, slots[1, step - 1])
+
+    mine = pl.ds(pl.multiple_of(core * seq, seq), seq)
+    theirs = pl.ds(pl.multiple_of((1 - core) * seq, seq), seq)
+    pair = remote(acc.at[:, theirs, :], part, pair_send.at[0], pair_recv.at[0], sibling)
+    pair.wait_recv()
+    kv_heads = width // HD
+    group = HEADS // KV_HEADS
+    for kind in range(2):
+        total = (acc[kind, mine, :] + part[kind]).astype(jnp.bfloat16)
+        for head in range(kv_heads):
+            kv[kind, head] = total[:, head * HD:(head + 1) * HD]
+
+    scale = HD ** (-0.5)
+    allowed = (lax.broadcasted_iota(jnp.int32, (seq, seq), 0)
+               >= lax.broadcasted_iota(jnp.int32, (seq, seq), 1))
+
+    def attend(head, carry):
+        keys = kv[0, head]
+        values = kv[1, head]
+        gradient = None
+        for member in range(group):
+            lanes = pl.ds(pl.multiple_of((head * group + member) * HD, HD), HD)
+            query = queries[:, lanes]
+            scores = jnp.where(allowed, dot_nt(query, keys) * scale, -1e30)
+            weights = jnp.exp(scores - jnp.max(scores, axis=-1, keepdims=True))
+            probs = (weights / jnp.sum(weights, axis=-1, keepdims=True)).astype(jnp.bfloat16)
+            attention[:, lanes] = dot(probs, values).astype(jnp.bfloat16)
+            prob_grad = dot_nt(cotangent[:, lanes], values)
+            wide = probs.astype(jnp.float32)
+            delta = jnp.sum(wide * prob_grad, axis=-1, keepdims=True)
+            score_grad = (wide * (prob_grad - delta) * scale).astype(jnp.bfloat16)
+            term = dot_tn(score_grad, query)
+            gradient = term if gradient is None else gradient + term
+        rows_grad[mine, pl.ds(pl.multiple_of(head * HD, HD), HD)] = gradient.astype(jnp.bfloat16)
+        return carry
+
+    lax.fori_loop(0, kv_heads, attend, 0)
+    swap = remote(rows_grad.at[mine], rows_grad.at[mine], pair_send.at[1], pair_recv.at[1], sibling)
+    swap.wait_recv()
+
+    half = width // 2
+
+    def term_of(way, position):
+        return dot_tn(act[block_at(position)], rows_grad[:, way * half:(way + 1) * half])
+
+    ring_flight = {}
+    for step in range(steps):
+        terms = (term_of(0, spot - 1 - step), term_of(1, spot + 1 + step))
+        for sub in range(SUBS):
+            span = pl.ds(sub * cut, cut)
+            for way in range(2):
+                value = terms[way][sub * cut:(sub + 1) * cut]
+                if step == 0:
+                    sums[way, 0, span, :] = value
+                else:
+                    ring_flight[way, step - 1, sub].wait_recv()
+                    sums[way, step, span, :] = sums[way, step, span, :] + value
+                ring_flight[way, step, sub] = remote(
+                    sums.at[way, step, span], sums.at[way, step + 1, span],
+                    rs_send.at[way, step, sub], rs_recv.at[way, step, sub], onward[way])
+    terms = (term_of(0, spot), term_of(1, spot))
+    for sub in range(SUBS):
+        span = pl.ds(sub * cut, cut)
+        for way in range(2):
+            ring_flight[way, steps - 1, sub].wait_recv()
+            key_grad[span, way * half:(way + 1) * half] = (
+                sums[way, steps, span, :] + terms[way][sub * cut:(sub + 1) * cut])
+    for copy in [*flight.values(), *act_copies, pair, swap, *ring_flight.values()]:
+        copy.wait_send()
+
+
+def fused(ring, hidden_in, norm_gain, key_weight, value_weight, queries, out_cotangent):
+    features, width = key_weight.shape
+    own_rows = hidden_in.shape[0]
+    seq = 2 * own_rows
+    tokens = 2 * seq
+    steps = ring - 1
+    dma = pltpu.SemaphoreType.DMA
+    vmem = pl.BlockSpec(memory_space=pltpu.VMEM)
+    return pl.pallas_call(
+        functools.partial(kernel, ring),
+        out_shape=(
+            jax.ShapeDtypeStruct(queries.shape, jnp.bfloat16),
+            jax.ShapeDtypeStruct((features, width), jnp.float32),
+        ),
+        in_specs=[vmem] * 6,
+        out_specs=(vmem, vmem),
+        scratch_shapes=[
+            pltpu.VMEM((2, ring, own_rows, features), jnp.bfloat16),
+            pltpu.VMEM((ring, tokens, features), jnp.bfloat16),
+            pltpu.VMEM((2, steps, features, width), jnp.bfloat16),
+            pltpu.VMEM((2, tokens, width), jnp.float32),
+            pltpu.VMEM((2, seq, width), jnp.float32),
+            pltpu.VMEM((2, width // HD, seq, HD), jnp.bfloat16),
+            pltpu.VMEM((tokens, width), jnp.bfloat16),
+            pltpu.VMEM((2, ring, features, width // 2), jnp.float32),
+            dma((2, steps, SUBS)),
+            dma((2, steps, SUBS)),
+            dma((3,)),
+            dma((3,)),
+            dma,
+            dma((2,)),
+            dma((2,)),
+            dma((2, steps, SUBS)),
+            dma((2, steps, SUBS)),
+        ],
+        compiler_params=pltpu.CompilerParams(
+            collective_id=0, has_side_effects=True, vmem_limit_bytes=48 * 1024 * 1024
+        ),
+        cost_estimate=pl.CostEstimate(flops=4 * 10**9, bytes_accessed=4 * 10**6, transcendentals=0),
+    )(hidden_in, norm_gain.reshape(1, -1), key_weight, value_weight, queries, out_cotangent)
+
+
+def shard_body(mesh, hidden_in, norm_gain, key_weight, value_weight, queries, out_cotangent):
+    dp, node = mesh.shape["dp"], mesh.shape["node"]
+    features, width = key_weight.shape
+    own_rows = hidden_in.shape[0]
+    if (
+        node == 2
+        and dp % 4 == 0
+        and EARLY < dp // 2
+        and features % 256 == 0
+        and width % 256 == 0
+        and own_rows % 16 == 0
+        and queries.shape[0] == 2 * own_rows
+        and own_rows <= 256
+    ):
+        return fused(dp // 2, hidden_in, norm_gain, key_weight, value_weight, queries, out_cotangent)
+    return local(hidden_in, norm_gain, key_weight, value_weight, queries, out_cotangent)
+
+
 def solution(mesh):
     in_specs = (
         P(("dp", "node"), None),
@@ -96,4 +350,4 @@
         P("dp", "node"),
     )
     out_specs = (P("dp", "node"), P("dp", "node"))
-    return jax.shard_map(local, mesh=mesh, in_specs=in_specs, out_specs=out_specs, check_vma=False)
+    return jax.shard_map(functools.partial(shard_body, mesh), mesh=mesh, in_specs=in_specs, out_specs=out_specs, check_vma=False)

time: 282 us -> 104 us (0.37)
  waiting for transfers between devices: 235 us -> 0 us
  Pallas kernels: 0 us -> 95.9 us
  matrix products: 22.9 us -> 0 us
  between operations: 13.8 us -> 0.65 us
  other arithmetic: 4.03 us -> 0 us
    all_gather x3 -> x0, waiting for transfers between devices: 131 us -> none  [the longest x1 50.7 us: local(): value_sum = add_rows(lax.all_gather(value_weight, 'dp', axis=0, tiled=True))]
    reduce_scatter x1 -> x0, waiting for transfers between devices: 102 us -> none  [local(): lax.psum_scatter(lax.dot_general(normed, key_rows_grad, (((0,), (0,)), ((...]
    pallas_call x0 -> x1, Pallas kernels: none -> 95.9 us  [fused(): pl.pallas_call(functools.partial(kernel, ring), out_shape=(jax.ShapeDtype...]
    dot_general x6 -> x0, matrix products: 19.8 us -> none  [the longest x2 8.37 us: add_rows(): return jnp.dot(normed, shard_piece, preferred_element_type=jnp.float32)]
    unnamed x9 -> x14, local copies, waits for them, and re-layouts: 1.02 us -> 7.5 us
    reshape x4 -> x0, local copies, waits for them, and re-layouts: 4.33 us -> none  [the longest x1 1.7 us: local(): key_proj = key_sum.astype(jnp.bfloat16).reshape(seq_rows, kv_local, HD)]
    sub x1 -> x0, matrix products: 3.06 us -> none  [local(): weights = jnp.exp(scores - row_max)]
  transfers between devices with their start and end apart: 4 -> 0, of which waited for: 4 -> 0; matrix products, arithmetic and copies ran while one was open for 4% -> 0% of each run, Pallas kernels for 0% -> 0%
where the time goes in v1:
time: 104 us
  Pallas kernels  95.9 us (92%)
  local copies, waits for them, and re-layouts  7.5 us (7%)
    pallas_call x1, Pallas kernels, fused(): pl.pallas_call(functools.partial(kernel, ring), out_shape=(jax.ShapeDtype...  95.9 us
    unnamed x14, local copies, waits for them, and re-layouts  7.5 us

profile of v1, /device:TPU:0, one launch (start us, length us, event | category | flops | bytes accessed | tf_op | source)
XLA Modules:
  0.0 104.1 jit_solution(2574939749324463581)
XLA Ops:
  0.6 0.0 copy-start
  0.6 1.2 %copy-done = bf16[128,4096]{1,0:T(8,128)(2,1)S(1)} copy-done((bf16[128,4096]{1,0:T(8,128)(2,1)S(1)}, bf16[128,4096]{1,0:T(8,128)(2,1)}, u32[]{:S(2)}) %copy-start) | copy-done | bytes 1048600
  1.9 0.0 copy-start.1
  1.9 1.0 copy-done.1
  2.9 0.0 copy-start.2
  2.9 1.0 copy-done.2
  3.9 0.0 copy-start.3
  3.9 0.9 copy-done.3
  4.9 0.0 copy-start.4
  4.9 0.9 copy-done.4
  5.8 0.0 copy-start.5
  5.8 0.7 copy-done.5
  6.6 95.9 %shard_map.77 = (bf16[256,1024]{1,0:T(8,128)(2,1)S(1)}, f32[256,512]{1,0:T(8,128)S(1)}) custom-call(bf16[128,4096]{1,0:T(8,128)(2,1)S(1)} %copy-done, f32[1,4096]{1,0:T(1,128)S(1)} %bitcast.1, bf16[256,512]{1,0:T(8,128)(2,1)S(1)} %copy-done.3, bf16[256,512]{1,0:T(8,128)(2,1)S(1)} %copy-done.4, bf16[256,1024]{1,0:T(8,128)(2,1)S(1)} %copy-done.1, ...), custom_call_target="tpu_custom_call" | custom-call | flops 4000000000 | bytes 4000000 | tf_op jit(solution)/shard_map/pallas_call | solution.py:291
  102.5 0.8 copy.10
  103.3 0.8 copy.11
Async XLA Ops:
  0.6 1.2 %copy-start = (bf16[128,4096]{1,0:T(8,128)(2,1)S(1)}, bf16[128,4096]{1,0:T(8,128)(2,1)}, u32[]{:S(2)}) copy-start(bf16[128,4096]{1,0:T(8,128)(2,1)} %hidden.1) | copy-start | bytes 3145732
  1.9 1.0 %copy-start.1 = (bf16[256,1024]{1,0:T(8,128)(2,1)S(1)}, bf16[256,1024]{1,0:T(8,128)(2,1)}, u32[]{:S(2)}) copy-start(bf16[256,1024]{1,0:T(8,128)(2,1)} %queries.1) | copy-start | bytes 1572868
  2.9 1.0 %copy-start.2 = (bf16[256,1024]{1,0:T(8,128)(2,1)S(1)}, bf16[256,1024]{1,0:T(8,128)(2,1)}, u32[]{:S(2)}) copy-start(bf16[256,1024]{1,0:T(8,128)(2,1)} %cotangent.1) | copy-start | bytes 1572868
  3.9 0.9 copy-start.3
  4.9 0.9 copy-start.4
  5.8 0.7 copy-start.5

commit v2 on v1

--- a/solution.py
+++ b/solution.py
@@ -91,7 +91,7 @@
 
 
 SUBS = 2
-EARLY = 5
+EARLY_B = 2
 
 
 def dot(a, b):
@@ -106,10 +106,10 @@
     return lax.dot_general(a, b, (((0,), (0,)), ((), ())), preferred_element_type=jnp.float32)
 
 
-def kernel(ring, hidden, gain, kw, vw, queries, cotangent, attention, key_grad,
-           stage, act, slots, acc, part, kv, rows_grad, sums,
-           ag_send, ag_recv, act_send, act_recv, act_local, pair_send, pair_recv,
-           rs_send, rs_recv):
+def kernel(ring, hidden_in, gain, kw, vw, queries_in, cotangent_in, attention, key_grad,
+           hidden, own, queries, cotangent, stage, act, slots, acc, part, kv, rows_grad, sums, terms,
+           in_sem, ag_send, ag_recv, act_send, act_recv, act_local, pair_send, pair_recv,
+           swap_send, swap_recv, rs_send, rs_recv):
     depth = ring // 2
     steps = ring - 1
     dp = lax.axis_index("dp")
@@ -126,6 +126,9 @@
         level = position * (1 - side) + (2 * depth - 1 - position) * side
         return level * 2 + side
 
+    def position_of(way, step):
+        return spot - step if way == 0 else spot + step
+
     right = (block_at(spot + 1) * 2 + core, node)
     left = (block_at(spot - 1) * 2 + core, node)
     sibling = (block * 2 + 1 - core, node)
@@ -133,6 +136,16 @@
     across = (block * 2 + 1 - core, 1 - node)
     mesh_ids = pl.DeviceIdType.MESH
 
+    loads = [
+        pltpu.make_async_copy(hidden_in, hidden, in_sem.at[0]),
+        pltpu.make_async_copy(kw, own.at[0], in_sem.at[1]),
+        pltpu.make_async_copy(vw, own.at[1], in_sem.at[2]),
+        pltpu.make_async_copy(queries_in, queries, in_sem.at[3]),
+        pltpu.make_async_copy(cotangent_in, cotangent, in_sem.at[4]),
+    ]
+    for load in loads:
+        load.start()
+
     barrier = pltpu.get_barrier_semaphore()
     for peer in (right, left, sibling, beside, across):
         pl.semaphore_signal(barrier, inc=1, device_id=peer, device_id_type=mesh_ids)
@@ -148,23 +161,28 @@
     onward = (right, left)
     features = kw.shape[0]
     width = kw.shape[1]
+    half = width // 2
     cut = features // SUBS
-    started = []
-
-    def gather_copy(way, step, sub):
+    flight = {}
+
+    def gather_copy(part_id, step, sub, way):
         span = pl.ds(sub * cut, cut)
-        source = (kw, vw)[way].at[span] if step == 0 else slots.at[way, step - 1, span]
-        return remote(source, slots.at[way, step, span], ag_send.at[way, step, sub],
-                      ag_recv.at[way, step, sub], onward[way])
-
-    flight = {}
+        if step == 0:
+            source = (kw, vw)[way].at[span, pl.ds(part_id * half, half)]
+        else:
+            source = slots.at[part_id, way, step - 1, span]
+        flight[part_id, step, sub, way] = remote(
+            source, slots.at[part_id, way, step, span], ag_send.at[part_id, way, step, sub],
+            ag_recv.at[part_id, way, step, sub], onward[way])
+
     for sub in range(SUBS):
         for way in range(2):
-            flight[way, 0, sub] = gather_copy(way, 0, sub)
+            gather_copy(0, 0, sub, way)
 
     own_rows = hidden.shape[0]
     seq = 2 * own_rows
     strip = 16
+    loads[0].wait()
 
     def normalize(index, carry):
         rows = pl.ds(pl.multiple_of(index * strip, strip), strip)
@@ -183,100 +201,177 @@
                                  act_recv.at[relation], peer))
     local_copy = pltpu.make_async_copy(stage.at[core], act.at[:, my_rows, :], act_local)
     local_copy.start()
-
-    def add_block(way, position, weight):
-        acc[way] = acc[way] + dot(act[block_at(position)], weight)
-
-    for step in range(1, steps + 1):
-        for sub in range(SUBS):
-            for way in range(2):
-                flight[way, step - 1, sub].wait_recv()
-                if step < steps:
-                    flight[way, step, sub] = gather_copy(way, step, sub)
-        if step == EARLY:
-            local_copy.wait()
-            for copy in act_copies:
-                copy.wait_recv()
-            acc[0] = dot(act[block], kw[...])
-            acc[1] = dot(act[block], vw[...])
-
-            def earlier(index, carry):
-                add_block(0, spot - 1 - index, slots[0, index])
-                add_block(1, spot + 1 + index, slots[1, index])
-                return carry
-
-            lax.fori_loop(0, EARLY, earlier, 0)
-        if step > EARLY:
-            add_block(0, spot - step, slots[0, step - 1])
-            add_block(1, spot + step, slots[1, step - 1])
+    for load in loads[1:]:
+        load.wait()
 
     mine = pl.ds(pl.multiple_of(core * seq, seq), seq)
     theirs = pl.ds(pl.multiple_of((1 - core) * seq, seq), seq)
-    pair = remote(acc.at[:, theirs, :], part, pair_send.at[0], pair_recv.at[0], sibling)
-    pair.wait_recv()
-    kv_heads = width // HD
+    heads_half = half // HD
     group = HEADS // KV_HEADS
-    for kind in range(2):
-        total = (acc[kind, mine, :] + part[kind]).astype(jnp.bfloat16)
-        for head in range(kv_heads):
-            kv[kind, head] = total[:, head * HD:(head + 1) * HD]
-
     scale = HD ** (-0.5)
-    allowed = (lax.broadcasted_iota(jnp.int32, (seq, seq), 0)
-               >= lax.broadcasted_iota(jnp.int32, (seq, seq), 1))
-
-    def attend(head, carry):
-        keys = kv[0, head]
-        values = kv[1, head]
-        gradient = None
-        for member in range(group):
-            lanes = pl.ds(pl.multiple_of((head * group + member) * HD, HD), HD)
-            query = queries[:, lanes]
-            scores = jnp.where(allowed, dot_nt(query, keys) * scale, -1e30)
-            weights = jnp.exp(scores - jnp.max(scores, axis=-1, keepdims=True))
-            probs = (weights / jnp.sum(weights, axis=-1, keepdims=True)).astype(jnp.bfloat16)
-            attention[:, lanes] = dot(probs, values).astype(jnp.bfloat16)
-            prob_grad = dot_nt(cotangent[:, lanes], values)
-            wide = probs.astype(jnp.float32)
-            delta = jnp.sum(wide * prob_grad, axis=-1, keepdims=True)
-            score_grad = (wide * (prob_grad - delta) * scale).astype(jnp.bfloat16)
-            term = dot_tn(score_grad, query)
-            gradient = term if gradient is None else gradient + term
-        rows_grad[mine, pl.ds(pl.multiple_of(head * HD, HD), HD)] = gradient.astype(jnp.bfloat16)
-        return carry
-
-    lax.fori_loop(0, kv_heads, attend, 0)
-    swap = remote(rows_grad.at[mine], rows_grad.at[mine], pair_send.at[1], pair_recv.at[1], sibling)
-    swap.wait_recv()
-
-    half = width // 2
-
-    def term_of(way, position):
-        return dot_tn(act[block_at(position)], rows_grad[:, way * half:(way + 1) * half])
-
-    ring_flight = {}
-    for step in range(steps):
-        terms = (term_of(0, spot - 1 - step), term_of(1, spot + 1 + step))
+    pairs, swaps = {}, {}
+    sum_flight = {}
+
+    def arrived_activations():
+        local_copy.wait()
+        for copy in act_copies:
+            copy.wait_recv()
+
+    def project_own(part_id):
+        lanes = slice(part_id * half, (part_id + 1) * half)
+        for way in range(2):
+            acc[part_id, way] = dot(act[block], own[way, :, lanes])
+
+    def project(part_id, step):
+        for way in range(2):
+            acc[part_id, way] = acc[part_id, way] + dot(
+                act[block_at(position_of(way, step))], slots[part_id, way, step - 1])
+
+    def send_pair(part_id):
+        pairs[part_id] = remote(acc.at[part_id, :, theirs, :], part.at[part_id],
+                                pair_send.at[part_id], pair_recv.at[part_id], sibling)
+
+    def take_pair(part_id):
+        pairs[part_id].wait_recv()
+        for kind in range(2):
+            total = (acc[part_id, kind, mine, :] + part[part_id, kind]).astype(jnp.bfloat16)
+            for head in range(heads_half):
+                kv[part_id, kind, head] = total[:, head * HD:(head + 1) * HD]
+
+    key_terms = {}
+
+    def attend(part_id, head, member):
+        keys = kv[part_id, 0, head]
+        values = kv[part_id, 1, head]
+        first = ((part_id * heads_half + head) * group + member) * HD
+        lanes = slice(first, first + HD)
+        allowed = (lax.broadcasted_iota(jnp.int32, (seq, seq), 0)
+                   >= lax.broadcasted_iota(jnp.int32, (seq, seq), 1))
+        query = queries[:, lanes]
+        scores = jnp.where(allowed, dot_nt(query, keys) * scale, -1e30)
+        weights = jnp.exp(scores - jnp.max(scores, axis=-1, keepdims=True))
+        probs = (weights / jnp.sum(weights, axis=-1, keepdims=True)).astype(jnp.bfloat16)
+        attention[:, lanes] = dot(probs, values).astype(jnp.bfloat16)
+        prob_grad = dot_nt(cotangent[:, lanes], values)
+        wide = probs.astype(jnp.float32)
+        delta = jnp.sum(wide * prob_grad, axis=-1, keepdims=True)
+        score_grad = (wide * (prob_grad - delta) * scale).astype(jnp.bfloat16)
+        term = dot_tn(score_grad, query)
+        if member > 0:
+            term = term + key_terms.pop((part_id, head))
+        if member < group - 1:
+            key_terms[part_id, head] = term
+        else:
+            rows_grad[part_id, mine, head * HD:(head + 1) * HD] = term.astype(jnp.bfloat16)
+
+    def send_swap(part_id):
+        swaps[part_id] = remote(rows_grad.at[part_id, mine], rows_grad.at[part_id, mine],
+                                swap_send.at[part_id], swap_recv.at[part_id], sibling)
+
+    share = features // 2
+    rows_cut = share // SUBS
+
+    def make_terms(part_id, step):
+        for way in range(2):
+            position = position_of(way, 1 + step)
+            terms[part_id, way] = dot_tn(
+                act[block_at(position), :, way * share:(way + 1) * share], rows_grad[part_id])
+
+    def sum_copy(part_id, step, sub, way):
+        span = pl.ds(sub * rows_cut, rows_cut)
+        sum_flight[part_id, step, sub, way] = remote(
+            sums.at[part_id, way, step, span], sums.at[part_id, way, step + 1, span],
+            rs_send.at[part_id, way, step, sub], rs_recv.at[part_id, way, step, sub], onward[way])
+
+    def start_sums(part_id):
+        swaps[part_id].wait_recv()
+        make_terms(part_id, 0)
         for sub in range(SUBS):
-            span = pl.ds(sub * cut, cut)
+            span = slice(sub * rows_cut, (sub + 1) * rows_cut)
             for way in range(2):
-                value = terms[way][sub * cut:(sub + 1) * cut]
-                if step == 0:
-                    sums[way, 0, span, :] = value
-                else:
-                    ring_flight[way, step - 1, sub].wait_recv()
-                    sums[way, step, span, :] = sums[way, step, span, :] + value
-                ring_flight[way, step, sub] = remote(
-                    sums.at[way, step, span], sums.at[way, step + 1, span],
-                    rs_send.at[way, step, sub], rs_recv.at[way, step, sub], onward[way])
-    terms = (term_of(0, spot), term_of(1, spot))
-    for sub in range(SUBS):
-        span = pl.ds(sub * cut, cut)
-        for way in range(2):
-            ring_flight[way, steps - 1, sub].wait_recv()
-            key_grad[span, way * half:(way + 1) * half] = (
-                sums[way, steps, span, :] + terms[way][sub * cut:(sub + 1) * cut])
-    for copy in [*flight.values(), *act_copies, pair, swap, *ring_flight.values()]:
+                sums[part_id, way, 0, span, :] = terms[part_id, way, span, :]
+                sum_copy(part_id, 0, sub, way)
+        make_terms(part_id, 1)
+
+    def gather_event(part_id, step, sub):
+        for way in range(2):
+            flight[part_id, step - 1, sub, way].wait_recv()
+            if step < steps:
+                gather_copy(part_id, step, sub, way)
+            if part_id == 0 and step == steps - 1:
+                gather_copy(1, 0, sub, way)
+
+    def sum_event(part_id, step, sub):
+        span = slice(sub * rows_cut, (sub + 1) * rows_cut)
+        for way in range(2):
+            sum_flight[part_id, step - 1, sub, way].wait_recv()
+            value = sums[part_id, way, step, span, :] + terms[part_id, way, span, :]
+            if step < steps:
+                sums[part_id, way, step, span, :] = value
+                sum_copy(part_id, step, sub, way)
+            else:
+                first = way * share + sub * rows_cut
+                key_grad[first:first + rows_cut, part_id * half:(part_id + 1) * half] = value
+        if sub == SUBS - 1 and step < steps:
+            make_terms(part_id, step + 1)
+
+    def attend_tasks(part_id):
+        tasks = []
+        for head in range(heads_half):
+            for member in range(group):
+                tasks.append(functools.partial(attend, part_id, head, member))
+        first, last = tasks[0], tasks[-1]
+
+        def opening():
+            take_pair(part_id)
+            first()
+
+        def closing():
+            last()
+            send_swap(part_id)
+
+        return [opening, *tasks[1:-1], closing]
+
+    def run_events(event, part_id, first, last, tasks):
+        for step in range(first, last + 1):
+            for sub in range(SUBS):
+                event(part_id, step, sub)
+                if tasks:
+                    tasks.pop(0)()
+
+    run_events(gather_event, 0, 1, steps, [])
+    run_events(gather_event, 1, 1, EARLY_B, [])
+    arrived_activations()
+
+    def project_first():
+        project_own(0)
+        for step in range(1, depth):
+            project(0, step)
+
+    def project_rest():
+        for step in range(depth, steps + 1):
+            project(0, step)
+        send_pair(0)
+
+    def project_ahead():
+        project_own(1)
+        for step in range(1, EARLY_B + 1):
+            project(1, step)
+
+    tasks = [project_first, project_rest, project_ahead, *attend_tasks(0)]
+    tasks.append(functools.partial(start_sums, 0))
+    run_events(gather_event, 1, EARLY_B + 1, steps, tasks)
+    for task in tasks:
+        task()
+    for step in range(EARLY_B + 1, steps + 1):
+        project(1, step)
+    send_pair(1)
+    tasks = [lambda: None, *attend_tasks(1), functools.partial(start_sums, 1)]
+    run_events(sum_event, 0, 1, steps, tasks)
+    for task in tasks:
+        task()
+    run_events(sum_event, 1, 1, steps, [])
+    for copy in [*flight.values(), *act_copies, *pairs.values(), *swaps.values(), *sum_flight.values()]:
         copy.wait_send()
 
 
@@ -286,37 +381,47 @@
     seq = 2 * own_rows
     tokens = 2 * seq
     steps = ring - 1
+    half = width // 2
     dma = pltpu.SemaphoreType.DMA
     vmem = pl.BlockSpec(memory_space=pltpu.VMEM)
+    anywhere = pl.BlockSpec(memory_space=pl.ANY)
     return pl.pallas_call(
         functools.partial(kernel, ring),
         out_shape=(
             jax.ShapeDtypeStruct(queries.shape, jnp.bfloat16),
             jax.ShapeDtypeStruct((features, width), jnp.float32),
         ),
-        in_specs=[vmem] * 6,
+        in_specs=[anywhere, vmem, anywhere, anywhere, anywhere, anywhere],
         out_specs=(vmem, vmem),
         scratch_shapes=[
+            pltpu.VMEM(hidden_in.shape, jnp.bfloat16),
+            pltpu.VMEM((2, features, width), jnp.bfloat16),
+            pltpu.VMEM(queries.shape, jnp.bfloat16),
+            pltpu.VMEM(queries.shape, jnp.bfloat16),
             pltpu.VMEM((2, ring, own_rows, features), jnp.bfloat16),
             pltpu.VMEM((ring, tokens, features), jnp.bfloat16),
-            pltpu.VMEM((2, steps, features, width), jnp.bfloat16),
-            pltpu.VMEM((2, tokens, width), jnp.float32),
-            pltpu.VMEM((2, seq, width), jnp.float32),
-            pltpu.VMEM((2, width // HD, seq, HD), jnp.bfloat16),
-            pltpu.VMEM((tokens, width), jnp.bfloat16),
-            pltpu.VMEM((2, ring, features, width // 2), jnp.float32),
-            dma((2, steps, SUBS)),
-            dma((2, steps, SUBS)),
+            pltpu.VMEM((2, 2, steps, features, half), jnp.bfloat16),
+            pltpu.VMEM((2, 2, tokens, half), jnp.float32),
+            pltpu.VMEM((2, 2, seq, half), jnp.float32),
+            pltpu.VMEM((2, 2, half // HD, seq, HD), jnp.bfloat16),
+            pltpu.VMEM((2, tokens, half), jnp.bfloat16),
+            pltpu.VMEM((2, 2, ring, features // 2, half), jnp.float32),
+            pltpu.VMEM((2, 2, features // 2, half), jnp.float32),
+            dma((5,)),
+            dma((2, 2, steps, SUBS)),
+            dma((2, 2, steps, SUBS)),
             dma((3,)),
             dma((3,)),
             dma,
             dma((2,)),
             dma((2,)),
-            dma((2, steps, SUBS)),
-            dma((2, steps, SUBS)),
+            dma((2,)),
+            dma((2,)),
+            dma((2, 2, steps, SUBS)),
+            dma((2, 2, steps, SUBS)),
         ],
         compiler_params=pltpu.CompilerParams(
-            collective_id=0, has_side_effects=True, vmem_limit_bytes=48 * 1024 * 1024
+            collective_id=0, has_side_effects=True, vmem_limit_bytes=58 * 1024 * 1024
         ),
         cost_estimate=pl.CostEstimate(flops=4 * 10**9, bytes_accessed=4 * 10**6, transcendentals=0),
     )(hidden_in, norm_gain.reshape(1, -1), key_weight, value_weight, queries, out_cotangent)
@@ -329,9 +434,9 @@
     if (
         node == 2
         and dp % 4 == 0
-        and EARLY < dp // 2
+        and EARLY_B + 1 < dp // 2
         and features % 256 == 0
-        and width % 256 == 0
+        and width % (4 * HD) == 0
         and own_rows % 16 == 0
         and queries.shape[0] == 2 * own_rows
         and own_rows <= 256

time: 104 us -> 115 us (1.11)
  Pallas kernels: 95.9 us -> 111 us
  local copies, waits for them, and re-layouts: 7.5 us -> 2.72 us
    pallas_call x1, Pallas kernels: 95.9 us -> 111 us  [fused(): pl.pallas_call(functools.partial(kernel, ring), out_shape=(jax.ShapeDtype...]
    unnamed x14 -> x4, local copies, waits for them, and re-layouts: 7.5 us -> 2.72 us
where the time goes in v2:
time: 115 us; the launch traced here: 114 us
  Pallas kernels  111 us (97%)
  local copies, waits for them, and re-layouts  2.72 us (2%)
    pallas_call x1, Pallas kernels, fused(): pl.pallas_call(functools.partial(kernel, ring), out_shape=(jax.ShapeDtype...  111 us
    unnamed x4, local copies, waits for them, and re-layouts  2.72 us

profile of v2, /device:TPU:0, one launch (start us, length us, event | category | flops | bytes accessed | tf_op | source)
XLA Modules:
  0.0 114.4 jit_solution(15367480860137508536)
XLA Ops:
  0.6 111.0 %shard_map.77 = (bf16[256,1024]{1,0:T(8,128)(2,1)}, f32[256,512]{1,0:T(8,128)}) custom-call(bf16[128,4096]{1,0:T(8,128)(2,1)} %hidden_in.1, f32[1,4096]{1,0:T(1,128)} %bitcast.1, bf16[256,512]{1,0:T(8,128)(2,1)} %kw.1, bf16[256,512]{1,0:T(8,128)(2,1)} %vw.1, bf16[256,1024]{1,0:T(8,128)(2,1)} %queries_in.1, bf16[256,1024]{1,0:T(8,128)(2,1)} %cotangent_in.1), custom_call_target="tpu_custom_call" | custom-call | flops 4000000000 | bytes 4000000 | tf_op jit(solution)/shard_map/pallas_call | solution.py:388
  111.6 0.0 copy-start
  111.6 1.9 %copy.10 = bf16[256,1024]{1,0:T(8,128)(2,1)} copy(bf16[256,1024]{1,0:T(8,128)(2,1)} %get-tuple-element.4) | data formatting | bytes 1048576
  113.6 0.0 copy-done
  113.6 0.8 copy.11
Async XLA Ops:
  111.6 1.9 %copy-start = (f32[256,512]{1,0:T(8,128)S(1)}, f32[256,512]{1,0:T(8,128)}, u32[]{:S(2)}) copy-start(f32[256,512]{1,0:T(8,128)} %get-tuple-element.5) | copy-start | bytes 1572868

commit v3 on v1

--- a/solution.py
+++ b/solution.py
@@ -106,9 +106,9 @@
     return lax.dot_general(a, b, (((0,), (0,)), ((), ())), preferred_element_type=jnp.float32)
 
 
-def kernel(ring, hidden, gain, kw, vw, queries, cotangent, attention, key_grad,
-           stage, act, slots, acc, part, kv, rows_grad, sums,
-           ag_send, ag_recv, act_send, act_recv, act_local, pair_send, pair_recv,
+def kernel(ring, hidden_in, gain, kw, vw, queries_in, cotangent_in, attention, key_grad,
+           hidden, own, queries, cotangent, stage, act, slots, acc, part, kv, rows_grad, sums,
+           in_sem, ag_send, ag_recv, act_send, act_recv, act_local, pair_send, pair_recv,
            rs_send, rs_recv):
     depth = ring // 2
     steps = ring - 1
@@ -133,6 +133,16 @@
     across = (block * 2 + 1 - core, 1 - node)
     mesh_ids = pl.DeviceIdType.MESH
 
+    loads = [
+        pltpu.make_async_copy(hidden_in, hidden, in_sem.at[0]),
+        pltpu.make_async_copy(kw, own.at[0], in_sem.at[1]),
+        pltpu.make_async_copy(vw, own.at[1], in_sem.at[2]),
+        pltpu.make_async_copy(queries_in, queries, in_sem.at[3]),
+        pltpu.make_async_copy(cotangent_in, cotangent, in_sem.at[4]),
+    ]
+    for load in loads:
+        load.start()
+
     barrier = pltpu.get_barrier_semaphore()
     for peer in (right, left, sibling, beside, across):
         pl.semaphore_signal(barrier, inc=1, device_id=peer, device_id_type=mesh_ids)
@@ -165,6 +175,7 @@
     own_rows = hidden.shape[0]
     seq = 2 * own_rows
     strip = 16
+    loads[0].wait()
 
     def normalize(index, carry):
         rows = pl.ds(pl.multiple_of(index * strip, strip), strip)
@@ -183,6 +194,8 @@
                                  act_recv.at[relation], peer))
     local_copy = pltpu.make_async_copy(stage.at[core], act.at[:, my_rows, :], act_local)
     local_copy.start()
+    for load in loads[1:]:
+        load.wait()
 
     def add_block(way, position, weight):
         acc[way] = acc[way] + dot(act[block_at(position)], weight)
@@ -197,8 +210,8 @@
             local_copy.wait()
             for copy in act_copies:
                 copy.wait_recv()
-            acc[0] = dot(act[block], kw[...])
-            acc[1] = dot(act[block], vw[...])
+            acc[0] = dot(act[block], own[0])
+            acc[1] = dot(act[block], own[1])
 
             def earlier(index, carry):
                 add_block(0, spot - 1 - index, slots[0, index])
@@ -245,7 +258,7 @@
         rows_grad[mine, pl.ds(pl.multiple_of(head * HD, HD), HD)] = gradient.astype(jnp.bfloat16)
         return carry
 
-    lax.fori_loop(0, kv_heads, attend, 0)
+    lax.fori_loop(0, kv_heads, attend, 0, unroll=True)
     swap = remote(rows_grad.at[mine], rows_grad.at[mine], pair_send.at[1], pair_recv.at[1], sibling)
     swap.wait_recv()
 
@@ -288,15 +301,20 @@
     steps = ring - 1
     dma = pltpu.SemaphoreType.DMA
     vmem = pl.BlockSpec(memory_space=pltpu.VMEM)
+    anywhere = pl.BlockSpec(memory_space=pl.ANY)
     return pl.pallas_call(
         functools.partial(kernel, ring),
         out_shape=(
             jax.ShapeDtypeStruct(queries.shape, jnp.bfloat16),
             jax.ShapeDtypeStruct((features, width), jnp.float32),
         ),
-        in_specs=[vmem] * 6,
+        in_specs=[anywhere, vmem, anywhere, anywhere, anywhere, anywhere],
         out_specs=(vmem, vmem),
         scratch_shapes=[
+            pltpu.VMEM(hidden_in.shape, jnp.bfloat16),
+            pltpu.VMEM((2, features, width), jnp.bfloat16),
+            pltpu.VMEM(queries.shape, jnp.bfloat16),
+            pltpu.VMEM(queries.shape, jnp.bfloat16),
             pltpu.VMEM((2, ring, own_rows, features), jnp.bfloat16),
             pltpu.VMEM((ring, tokens, features), jnp.bfloat16),
             pltpu.VMEM((2, steps, features, width), jnp.bfloat16),
@@ -305,6 +323,7 @@
             pltpu.VMEM((2, width // HD, seq, HD), jnp.bfloat16),
             pltpu.VMEM((tokens, width), jnp.bfloat16),
             pltpu.VMEM((2, ring, features, width // 2), jnp.float32),
+            dma((5,)),
             dma((2, steps, SUBS)),
             dma((2, steps, SUBS)),
             dma((3,)),
@@ -316,7 +335,7 @@
             dma((2, steps, SUBS)),
         ],
         compiler_params=pltpu.CompilerParams(
-            collective_id=0, has_side_effects=True, vmem_limit_bytes=48 * 1024 * 1024
+            collective_id=0, has_side_effects=True, vmem_limit_bytes=58 * 1024 * 1024
         ),
         cost_estimate=pl.CostEstimate(flops=4 * 10**9, bytes_accessed=4 * 10**6, transcendentals=0),
     )(hidden_in, norm_gain.reshape(1, -1), key_weight, value_weight, queries, out_cotangent)

time: 104 us -> 102 us (0.981)
  local copies, waits for them, and re-layouts: 7.5 us -> 2.72 us
  Pallas kernels: 95.9 us -> 98 us
    unnamed x14 -> x4, local copies, waits for them, and re-layouts: 7.5 us -> 2.72 us
    pallas_call x1, Pallas kernels: 95.9 us -> 98 us  [fused(): pl.pallas_call(functools.partial(kernel, ring), out_shape=(jax.ShapeDtype...]
where the time goes in v3:
time: 102 us; the launch traced here: 101 us
  Pallas kernels  98 us (96%)
  local copies, waits for them, and re-layouts  2.72 us (3%)
    pallas_call x1, Pallas kernels, fused(): pl.pallas_call(functools.partial(kernel, ring), out_shape=(jax.ShapeDtype...  98 us
    unnamed x4, local copies, waits for them, and re-layouts  2.72 us

profile of v3, /device:TPU:0, one launch (start us, length us, event | category | flops | bytes accessed | tf_op | source)
XLA Modules:
  0.0 101.4 jit_solution(11950606014591665611)
XLA Ops:
  0.6 98.0 %shard_map.77 = (bf16[256,1024]{1,0:T(8,128)(2,1)}, f32[256,512]{1,0:T(8,128)}) custom-call(bf16[128,4096]{1,0:T(8,128)(2,1)} %hidden_in.1, f32[1,4096]{1,0:T(1,128)} %bitcast.1, bf16[256,512]{1,0:T(8,128)(2,1)} %kw.1, bf16[256,512]{1,0:T(8,128)(2,1)} %vw.1, bf16[256,1024]{1,0:T(8,128)(2,1)} %queries_in.1, bf16[256,1024]{1,0:T(8,128)(2,1)} %cotangent_in.1), custom_call_target="tpu_custom_call" | custom-call | flops 4000000000 | bytes 4000000 | tf_op jit(solution)/shard_map/pallas_call | solution.py:305
  98.6 0.0 copy-start
  98.6 1.9 %copy.10 = bf16[256,1024]{1,0:T(8,128)(2,1)} copy(bf16[256,1024]{1,0:T(8,128)(2,1)} %get-tuple-element.4) | data formatting | bytes 1048576
  100.6 0.0 copy-done
  100.6 0.8 copy.11
Async XLA Ops:
  98.6 1.9 %copy-start = (f32[256,512]{1,0:T(8,128)S(1)}, f32[256,512]{1,0:T(8,128)}, u32[]{:S(2)}) copy-start(f32[256,512]{1,0:T(8,128)} %get-tuple-element.5) | copy-start | bytes 1572868

commit v4 on v3

--- a/solution.py
+++ b/solution.py
@@ -219,17 +219,21 @@
                 return carry
 
             lax.fori_loop(0, EARLY, earlier, 0)
-        if step > EARLY:
+        if EARLY < step < steps:
             add_block(0, spot - step, slots[0, step - 1])
             add_block(1, spot + step, slots[1, step - 1])
 
     mine = pl.ds(pl.multiple_of(core * seq, seq), seq)
     theirs = pl.ds(pl.multiple_of((1 - core) * seq, seq), seq)
-    pair = remote(acc.at[:, theirs, :], part, pair_send.at[0], pair_recv.at[0], sibling)
-    pair.wait_recv()
+    pairs = []
+    for kind, position in enumerate((spot - steps, spot + steps)):
+        add_block(kind, position, slots[kind, steps - 1])
+        pairs.append(remote(acc.at[kind, theirs, :], part.at[kind], pair_send.at[kind],
+                            pair_recv.at[kind], sibling))
     kv_heads = width // HD
     group = HEADS // KV_HEADS
     for kind in range(2):
+        pairs[kind].wait_recv()
         total = (acc[kind, mine, :] + part[kind]).astype(jnp.bfloat16)
         for head in range(kv_heads):
             kv[kind, head] = total[:, head * HD:(head + 1) * HD]
@@ -259,7 +263,7 @@
         return carry
 
     lax.fori_loop(0, kv_heads, attend, 0, unroll=True)
-    swap = remote(rows_grad.at[mine], rows_grad.at[mine], pair_send.at[1], pair_recv.at[1], sibling)
+    swap = remote(rows_grad.at[mine], rows_grad.at[mine], pair_send.at[2], pair_recv.at[2], sibling)
     swap.wait_recv()
 
     half = width // 2
@@ -289,7 +293,7 @@
             ring_flight[way, steps - 1, sub].wait_recv()
             key_grad[span, way * half:(way + 1) * half] = (
                 sums[way, steps, span, :] + terms[way][sub * cut:(sub + 1) * cut])
-    for copy in [*flight.values(), *act_copies, pair, swap, *ring_flight.values()]:
+    for copy in [*flight.values(), *act_copies, *pairs, swap, *ring_flight.values()]:
         copy.wait_send()
 
 
@@ -329,8 +333,8 @@
             dma((3,)),
             dma((3,)),
             dma,
-            dma((2,)),
-            dma((2,)),
+            dma((3,)),
+            dma((3,)),
             dma((2, steps, SUBS)),
             dma((2, steps, SUBS)),
         ],

time: 102 us -> 101 us (level)
  no operation moved by 1% of the time
where the time goes in v4:
time: 101 us
  Pallas kernels  97.9 us (97%)
  local copies, waits for them, and re-layouts  2.72 us (3%)
    pallas_call x1, Pallas kernels, fused(): pl.pallas_call(functools.partial(kernel, ring), out_shape=(jax.ShapeDtype...  97.9 us
    unnamed x4, local copies, waits for them, and re-layouts  2.72 us

profile of v4, /device:TPU:0, one launch (start us, length us, event | category | flops | bytes accessed | tf_op | source)
XLA Modules:
  0.0 101.2 jit_solution(6173576669412530276)
XLA Ops:
  0.6 97.9 %shard_map.77 = (bf16[256,1024]{1,0:T(8,128)(2,1)}, f32[256,512]{1,0:T(8,128)}) custom-call(bf16[128,4096]{1,0:T(8,128)(2,1)} %hidden_in.1, f32[1,4096]{1,0:T(1,128)} %bitcast.1, bf16[256,512]{1,0:T(8,128)(2,1)} %kw.1, bf16[256,512]{1,0:T(8,128)(2,1)} %vw.1, bf16[256,1024]{1,0:T(8,128)(2,1)} %queries_in.1, bf16[256,1024]{1,0:T(8,128)(2,1)} %cotangent_in.1), custom_call_target="tpu_custom_call" | custom-call | flops 4000000000 | bytes 4000000 | tf_op jit(solution)/shard_map/pallas_call | solution.py:309
  98.5 0.0 copy-start
  98.5 1.9 %copy.10 = bf16[256,1024]{1,0:T(8,128)(2,1)} copy(bf16[256,1024]{1,0:T(8,128)(2,1)} %get-tuple-element.4) | data formatting | bytes 1048576
  100.4 0.0 copy-done
  100.4 0.8 copy.11
Async XLA Ops:
  98.5 1.9 %copy-start = (f32[256,512]{1,0:T(8,128)S(1)}, f32[256,512]{1,0:T(8,128)}, u32[]{:S(2)}) copy-start(f32[256,512]{1,0:T(8,128)} %get-tuple-element.5) | copy-start | bytes 1572868

commit v5 on v2

--- a/solution.py
+++ b/solution.py
@@ -90,8 +90,8 @@
     return (jnp.concatenate(outputs, axis=0), key_grad)
 
 
-SUBS = 2
-EARLY_B = 2
+SUBS = 1
+EARLY = 5
 
 
 def dot(a, b):
@@ -175,9 +175,9 @@
             source, slots.at[part_id, way, step, span], ag_send.at[part_id, way, step, sub],
             ag_recv.at[part_id, way, step, sub], onward[way])
 
-    for sub in range(SUBS):
-        for way in range(2):
-            gather_copy(0, 0, sub, way)
+    for part_id in range(2):
+        for way in range(2):
+            gather_copy(part_id, 0, 0, way)
 
     own_rows = hidden.shape[0]
     seq = 2 * own_rows
@@ -298,8 +298,6 @@
             flight[part_id, step - 1, sub, way].wait_recv()
             if step < steps:
                 gather_copy(part_id, step, sub, way)
-            if part_id == 0 and step == steps - 1:
-                gather_copy(1, 0, sub, way)
 
     def sum_event(part_id, step, sub):
         span = slice(sub * rows_cut, (sub + 1) * rows_cut)
@@ -332,45 +330,41 @@
 
         return [opening, *tasks[1:-1], closing]
 
-    def run_events(event, part_id, first, last, tasks):
-        for step in range(first, last + 1):
-            for sub in range(SUBS):
-                event(part_id, step, sub)
-                if tasks:
-                    tasks.pop(0)()
-
-    run_events(gather_event, 0, 1, steps, [])
-    run_events(gather_event, 1, 1, EARLY_B, [])
-    arrived_activations()
-
-    def project_first():
+    def own_first():
+        arrived_activations()
         project_own(0)
-        for step in range(1, depth):
-            project(0, step)
-
-    def project_rest():
-        for step in range(depth, steps + 1):
-            project(0, step)
-        send_pair(0)
-
-    def project_ahead():
         project_own(1)
-        for step in range(1, EARLY_B + 1):
-            project(1, step)
-
-    tasks = [project_first, project_rest, project_ahead, *attend_tasks(0)]
-    tasks.append(functools.partial(start_sums, 0))
-    run_events(gather_event, 1, EARLY_B + 1, steps, tasks)
-    for task in tasks:
+
+    work = [own_first]
+    for step in range(1, steps - 1):
+        for part_id in range(2):
+            work.append(functools.partial(project, part_id, step))
+    for step in range(1, steps):
+        for part_id in range(2):
+            gather_event(part_id, step, 0)
+            if step >= EARLY:
+                for _ in range(3):
+                    if work:
+                        work.pop(0)()
+    for task in work:
         task()
-    for step in range(EARLY_B + 1, steps + 1):
-        project(1, step)
-    send_pair(1)
-    tasks = [lambda: None, *attend_tasks(1), functools.partial(start_sums, 1)]
-    run_events(sum_event, 0, 1, steps, tasks)
-    for task in tasks:
+    for part_id in range(2):
+        project(part_id, steps - 1)
+    for part_id in range(2):
+        gather_event(part_id, steps, 0)
+        project(part_id, steps)
+        send_pair(part_id)
+    for task in attend_tasks(0):
         task()
-    run_events(sum_event, 1, 1, steps, [])
+    second = attend_tasks(1)
+    second[0]()
+    start_sums(0)
+    for task in second[1:]:
+        task()
+    start_sums(1)
+    for step in range(1, steps + 1):
+        for part_id in range(2):
+            sum_event(part_id, step, 0)
     for copy in [*flight.values(), *act_copies, *pairs.values(), *swaps.values(), *sum_flight.values()]:
         copy.wait_send()
 
@@ -434,7 +428,7 @@
     if (
         node == 2
         and dp % 4 == 0
-        and EARLY_B + 1 < dp // 2
+        and EARLY + 2 < dp // 2
         and features % 256 == 0
         and width % (4 * HD) == 0
         and own_rows % 16 == 0

time: 115 us -> 96.7 us (0.84)
  Pallas kernels: 111 us -> 93.1 us
    pallas_call x1, Pallas kernels: 111 us -> 93.1 us  [fused(): pl.pallas_call(functools.partial(kernel, ring), out_shape=(jax.ShapeDtype...]
where the time goes in v5:
time: 96.7 us; the launch traced here: 96.5 us
  Pallas kernels  93.1 us (96%)
  local copies, waits for them, and re-layouts  2.72 us (3%)
    pallas_call x1, Pallas kernels, fused(): pl.pallas_call(functools.partial(kernel, ring), out_shape=(jax.ShapeDtype...  93.1 us
    unnamed x4, local copies, waits for them, and re-layouts  2.72 us

profile of v5, /device:TPU:0, one launch (start us, length us, event | category | flops | bytes accessed | tf_op | source)
XLA Modules:
  0.0 96.5 jit_solution(10955881170739970713)
XLA Ops:
  0.6 93.1 %shard_map.77 = (bf16[256,1024]{1,0:T(8,128)(2,1)}, f32[256,512]{1,0:T(8,128)}) custom-call(bf16[128,4096]{1,0:T(8,128)(2,1)} %hidden_in.1, f32[1,4096]{1,0:T(1,128)} %bitcast.1, bf16[256,512]{1,0:T(8,128)(2,1)} %kw.1, bf16[256,512]{1,0:T(8,128)(2,1)} %vw.1, bf16[256,1024]{1,0:T(8,128)(2,1)} %queries_in.1, bf16[256,1024]{1,0:T(8,128)(2,1)} %cotangent_in.1), custom_call_target="tpu_custom_call" | custom-call | flops 4000000000 | bytes 4000000 | tf_op jit(solution)/shard_map/pallas_call | solution.py:382
  93.8 0.0 copy-start
  93.8 1.9 %copy.10 = bf16[256,1024]{1,0:T(8,128)(2,1)} copy(bf16[256,1024]{1,0:T(8,128)(2,1)} %get-tuple-element.4) | data formatting | bytes 1048576
  95.7 0.0 copy-done
  95.7 0.8 copy.11
Async XLA Ops:
  93.8 1.9 %copy-start = (f32[256,512]{1,0:T(8,128)S(1)}, f32[256,512]{1,0:T(8,128)}, u32[]{:S(2)}) copy-start(f32[256,512]{1,0:T(8,128)} %get-tuple-element.5) | copy-start | bytes 1572868

commit v6 on v5

--- a/solution.py
+++ b/solution.py
@@ -106,8 +106,8 @@
     return lax.dot_general(a, b, (((0,), (0,)), ((), ())), preferred_element_type=jnp.float32)
 
 
-def kernel(ring, hidden_in, gain, kw, vw, queries_in, cotangent_in, attention, key_grad,
-           hidden, own, queries, cotangent, stage, act, slots, acc, part, kv, rows_grad, sums, terms,
+def kernel(ring, hidden_in, gain_in, kw, vw, queries_in, cotangent_in, attention, key_grad,
+           hidden, gain, own, queries, cotangent, stage, act, slots, acc, part, kv, rows_grad, sums, terms,
            in_sem, ag_send, ag_recv, act_send, act_recv, act_local, pair_send, pair_recv,
            swap_send, swap_recv, rs_send, rs_recv):
     depth = ring // 2
@@ -142,6 +142,7 @@
         pltpu.make_async_copy(vw, own.at[1], in_sem.at[2]),
         pltpu.make_async_copy(queries_in, queries, in_sem.at[3]),
         pltpu.make_async_copy(cotangent_in, cotangent, in_sem.at[4]),
+        pltpu.make_async_copy(gain_in, gain, in_sem.at[5]),
     ]
     for load in loads:
         load.start()
@@ -183,6 +184,7 @@
     seq = 2 * own_rows
     strip = 16
     loads[0].wait()
+    loads[5].wait()
 
     def normalize(index, carry):
         rows = pl.ds(pl.multiple_of(index * strip, strip), strip)
@@ -201,7 +203,7 @@
                                  act_recv.at[relation], peer))
     local_copy = pltpu.make_async_copy(stage.at[core], act.at[:, my_rows, :], act_local)
     local_copy.start()
-    for load in loads[1:]:
+    for load in loads[1:5]:
         load.wait()
 
     mine = pl.ds(pl.multiple_of(core * seq, seq), seq)
@@ -385,10 +387,11 @@
             jax.ShapeDtypeStruct(queries.shape, jnp.bfloat16),
             jax.ShapeDtypeStruct((features, width), jnp.float32),
         ),
-        in_specs=[anywhere, vmem, anywhere, anywhere, anywhere, anywhere],
+        in_specs=[anywhere] * 6,
         out_specs=(vmem, vmem),
         scratch_shapes=[
             pltpu.VMEM(hidden_in.shape, jnp.bfloat16),
+            pltpu.VMEM((1, hidden_in.shape[1]), jnp.float32),
             pltpu.VMEM((2, features, width), jnp.bfloat16),
             pltpu.VMEM(queries.shape, jnp.bfloat16),
             pltpu.VMEM(queries.shape, jnp.bfloat16),
@@ -401,7 +404,7 @@
             pltpu.VMEM((2, tokens, half), jnp.bfloat16),
             pltpu.VMEM((2, 2, ring, features // 2, half), jnp.float32),
             pltpu.VMEM((2, 2, features // 2, half), jnp.float32),
-            dma((5,)),
+            dma((6,)),
             dma((2, 2, steps, SUBS)),
             dma((2, 2, steps, SUBS)),
             dma((3,)),

time: 96.7 us -> 96 us (level)
  no operation moved by 1% of the time
where the time goes in v6:
time: 96 us; the launch traced here: 95.9 us
  Pallas kernels  92.5 us (96%)
  local copies, waits for them, and re-layouts  2.72 us (3%)
    pallas_call x1, Pallas kernels, fused(): pl.pallas_call(functools.partial(kernel, ring), out_shape=(jax.ShapeDtype...  92.5 us
    unnamed x4, local copies, waits for them, and re-layouts  2.72 us

profile of v6, /device:TPU:0, one launch (start us, length us, event | category | flops | bytes accessed | tf_op | source)
XLA Modules:
  0.0 95.9 jit_solution(5065529465544413664)
XLA Ops:
  0.6 92.5 %shard_map.77 = (bf16[256,1024]{1,0:T(8,128)(2,1)}, f32[256,512]{1,0:T(8,128)}) custom-call(bf16[128,4096]{1,0:T(8,128)(2,1)} %hidden_in.1, f32[1,4096]{1,0:T(1,128)} %bitcast.1, bf16[256,512]{1,0:T(8,128)(2,1)} %kw.1, bf16[256,512]{1,0:T(8,128)(2,1)} %vw.1, bf16[256,1024]{1,0:T(8,128)(2,1)} %queries_in.1, bf16[256,1024]{1,0:T(8,128)(2,1)} %cotangent_in.1), custom_call_target="tpu_custom_call" | custom-call | flops 4000000000 | bytes 4000000 | tf_op jit(solution)/shard_map/pallas_call | solution.py:384
  93.1 0.0 copy-start
  93.1 1.9 %copy.10 = bf16[256,1024]{1,0:T(8,128)(2,1)} copy(bf16[256,1024]{1,0:T(8,128)(2,1)} %get-tuple-element.4) | data formatting | bytes 1048576
  95.1 0.0 copy-done
  95.1 0.8 copy.11
Async XLA Ops:
  93.1 1.9 %copy-start = (f32[256,512]{1,0:T(8,128)S(1)}, f32[256,512]{1,0:T(8,128)}, u32[]{:S(2)}) copy-start(f32[256,512]{1,0:T(8,128)} %get-tuple-element.5) | copy-start | bytes 1572868
